TPU v7x, 32 devices: a whole 2x2x4 slice. The times are simulated.
32 devices in a mesh: groups: 2 (over y), blk: 8 (over z, x), inner: 2 (over core).
Axes of the slice: x: 2, y: 2, z: 4, core: 2. Of those that a mesh axis runs over, the one named last changes fastest.
Arguments:
- inputs: float32 [32, 32768], P(None, ('groups', 'blk')), parts along dimension 1, may hold values from -6 to 6
- solved: float32 [16, 32768], P('inner', ('groups', 'blk')), parts along dimension 1, may hold values from -3.5 to 3.5
- probes: float32 [16, 32768], P('inner', ('groups', 'blk')), parts along dimension 1, may hold values from -6 to 6
- task_factor: float32 [16, 8], P('groups'), parts along dimension 0, may hold values from -2 to 2
- inv_len: float32 [64], P('groups'), parts along dimension 0, may hold values from 0.06 to 0.3
Outputs:
- window_grad: float32 [32, 32768], P(None, ('groups', 'blk', 'inner')), parts along dimension 1
There are 2 independent parts, one for each index of `groups`. A program takes and returns all parts, laid end to end along the dimension named above; each array names one. Nothing has to cross between parts.
All inputs are finite; a program needn't handle non-finite values.
Results may differ from a plain program's by a relative error of at most 0.0003.
Values sent between devices are 32-bit elements; how exact they have to be, the bound alone decides.
A program may use at most 128 MiB of HBM per device.

v0:
```python
import functools
import math

import jax
import jax.numpy as jnp
from jax import lax
from jax.experimental import pallas as pl
from jax.experimental.pallas import tpu as pltpu
from jax.sharding import PartitionSpec as P

PROBES = 2
OFFSETS = (1, -1, 2, -2)
TI = 512
JC = 256
KDIM = 128
MESH = pl.DeviceIdType.MESH
ROOT = math.sqrt(math.log2(math.e))
F32 = jnp.float32
BF16 = jnp.bfloat16
precise = lax.Precision.HIGHEST


def split(value):
    high = value.astype(BF16).astype(F32)
    return high, (value - high).astype(BF16).astype(F32)


def split3(value):
    high = value.astype(BF16).astype(F32)
    rest = value - high
    mid = rest.astype(BF16).astype(F32)
    return high, mid, (rest - mid).astype(BF16).astype(F32)


def kernel(n_blk, x_ref, u_ref, v_ref, f_ref, len_ref, out_ref,
           xs, us, vs, own_u, own_v, a_exp, a_pair, b_exp, b_pair, b_y, acc, part, got,
           send_sem, recv_sem):
    grp = lax.axis_index("groups")
    blk = lax.axis_index("blk")
    me = lax.axis_index("inner")
    mate = 1 - me
    width, rows = x_ref.shape
    half = rows // 2
    tasks = u_ref.shape[0]

    barrier = pltpu.get_barrier_semaphore()
    pl.semaphore_signal(barrier, inc=1, device_id=(grp, blk, mate), device_id_type=MESH)
    for off in OFFSETS:
        other = lax.rem(blk + off + n_blk, n_blk)
        for inner in (me, mate):
            pl.semaphore_signal(barrier, inc=1, device_id=(grp, other, inner), device_id_type=MESH)
    pl.semaphore_wait(barrier, 1 + 2 * len(OFFSETS))

    def remote(src, dst, slot, kind, target):
        return pltpu.make_async_remote_copy(
            src_ref=src, dst_ref=dst, send_sem=send_sem.at[slot, kind], recv_sem=recv_sem.at[slot, kind],
            device_id=target, device_id_type=MESH)

    mine = pl.ds(pl.multiple_of(me * half, half), half)
    theirs = pl.ds(pl.multiple_of(mate * half, half), half)

    def copies(slot):
        far = len(OFFSETS)
        if isinstance(slot, int) and slot == far:
            partner = (grp, blk, mate)
            return [remote(u_ref, own_u.at[me], far, 0, partner), remote(v_ref, own_v.at[me], far, 1, partner)]
        target = lax.rem(blk - OFFSETS[slot] + n_blk, n_blk) if isinstance(slot, int) else lax.rem(blk + 1, n_blk)
        same, cross = (grp, target, me), (grp, target, mate)
        return [
            remote(x_ref.at[:, mine], xs.at[slot], slot, 0, same),
            remote(u_ref.at[:, mine], us.at[slot, me], slot, 1, same),
            remote(v_ref.at[:, mine], vs.at[slot, me], slot, 2, same),
            remote(u_ref.at[:, theirs], us.at[slot, me], slot, 3, cross),
            remote(v_ref.at[:, theirs], vs.at[slot, me], slot, 4, cross),
        ]

    partner_copies = copies(len(OFFSETS))
    for copy in partner_copies:
        copy.start()
    for slot in range(len(OFFSETS)):
        for copy in copies(slot):
            copy.start()

    own_u[me] = u_ref[...]
    own_v[me] = v_ref[...]
    square = (width, width)
    diag = lax.broadcasted_iota(jnp.int32, square, 0) == lax.broadcasted_iota(jnp.int32, square, 1)
    inv = jnp.sum(jnp.where(diag, jnp.broadcast_to(len_ref[...], square), 0.0), axis=1, keepdims=True)
    scale = inv * ROOT

    def norm_rows(y, ones_first):
        cols = y.shape[1]
        norm = jnp.broadcast_to(-0.5 * jnp.sum(y * y, axis=0, keepdims=True), (8, cols))
        high, mid, low = split3(norm)
        row = lax.broadcasted_iota(jnp.int32, (8, cols), 0)
        base = 3 if ones_first else 0
        ones = jnp.where((row < 3) if ones_first else (row >= 3) & (row < 6), 1.0, 0.0)
        picked = jnp.where(row == base, high, jnp.where(row == base + 1, mid, jnp.where(row == base + 2, low, ones)))
        return picked

    def prepare(slot, x, u0, u1, v0, v1):
        cols = x.shape[1]
        y = x * scale
        yh, yl = split(y)
        tail = jnp.zeros((KDIM - 3 * width - 8, cols), F32)
        b_exp[slot] = jnp.concatenate([yh, yl, yh, norm_rows(y, True), tail], axis=0).astype(BF16)
        one = jnp.where(lax.broadcasted_iota(jnp.int32, (16, cols), 0) == 0, 1.0, 0.0)
        b_y[slot] = jnp.concatenate([yh, yl, one], axis=0).astype(BF16)
        u = jnp.concatenate([u0, u1], axis=0)
        v = jnp.concatenate([v0, v1], axis=0)
        uh, ul = split(u)
        vh, vl = split(v)
        b_pair[slot] = jnp.concatenate([vh, vl, vh, uh, ul, uh], axis=0).astype(BF16)

    chunk = 512

    @pl.loop(0, rows // chunk)
    def _(index):
        at = pl.ds(pl.multiple_of(index * chunk, chunk), chunk)
        y = x_ref[:, at] * scale
        yh, yl = split(y)
        tail = jnp.zeros((KDIM - 3 * width - 8, chunk), F32)
        full = jnp.concatenate([yh, yh, yl, norm_rows(y, False), tail], axis=0)
        a_exp[at, :] = full.T.astype(BF16)

    factor = f_ref[...]
    cov = lax.dot_general(factor, factor, (((1,), (1,)), ((), ())), precision=precise, preferred_element_type=F32)

    for copy in partner_copies:
        copy.wait()

    def fold(ref, at):
        return jnp.concatenate(
            [jnp.dot(cov, ref[p, :, at], precision=precise, preferred_element_type=F32) for p in range(2)], axis=0)

    @pl.loop(0, rows // chunk)
    def _(index):
        at = pl.ds(pl.multiple_of(index * chunk, chunk), chunk)
        gh, gl = split(fold(own_u, at))
        wh, wl = split(fold(own_v, at))
        full = jnp.concatenate([gh, gh, gl, wh, wh, wl, jnp.zeros((KDIM - 12 * tasks, chunk), F32)], axis=0)
        a_pair[at, :] = full.T[:, : 12 * tasks].astype(BF16)

    def tiles(slot, first, start):
        @pl.loop(0, half // TI)
        def _(index):
            at = pl.ds(pl.multiple_of(start + index * TI, TI), TI)
            le = a_exp[at, :]
            lp = a_pair[at, :]
            total = None
            for c in range(half // JC):
                cols = pl.ds(c * JC, JC)
                expo = jnp.dot(le, b_exp[slot, :, cols], preferred_element_type=F32)
                pair = jnp.dot(lp, b_pair[slot, :, cols], preferred_element_type=F32)
                strength = jnp.exp2(expo) * pair
                high = strength.astype(BF16)
                low = (strength - high.astype(F32)).astype(BF16)
                right = b_y[slot, :, cols]
                dims = (((1,), (1,)), ((), ()))
                term = lax.dot_general(high, right, dims, preferred_element_type=F32)
                term = term + lax.dot_general(low, right, dims, preferred_element_type=F32)
                total = term if total is None else total + term
            if first:
                acc[at, :] = total
            else:
                acc[at, :] = acc[at, :] + total

    def gather(start):
        flat = acc[pl.ds(pl.multiple_of(start, half), half), :].T
        return flat[:width] + flat[width : 2 * width], flat[2 * width : 2 * width + 8]

    own = len(OFFSETS)
    prepare(own, x_ref[:, mine], own_u[0, :, mine], own_u[1, :, mine], own_v[0, :, mine], own_v[1, :, mine])
    tiles(own, True, mate * half)
    tiles(own, True, me * half)
    swap = remote(part, got, own, 2, (grp, blk, mate))
    for slot in range(len(OFFSETS)):
        for copy in copies(slot):
            copy.wait()
        prepare(slot, xs[slot], us[slot, 0], us[slot, 1], vs[slot, 0], vs[slot, 1])
        tiles(slot, False, mate * half)
        if slot == len(OFFSETS) - 1:
            moved, total = gather(mate * half)
            part[:width] = moved
            part[width:] = total
            swap.start()
        tiles(slot, False, me * half)
    moved, total = gather(me * half)
    swap.wait()
    moved = moved + got[:width]
    total = (total + got[width:])[:1]
    out_ref[...] = (inv * (-1.0 / (PROBES * ROOT))) * (x_ref[:, mine] * scale * total - moved)


def local(n_blk, inputs, solved, probes, task_factor, inv_len):
    width, rows = inputs.shape
    tasks = solved.shape[0]
    half = rows // 2
    near = len(OFFSETS)
    vmem = pl.BlockSpec(memory_space=pltpu.VMEM)
    pairs = 2 * rows * half * (2 * near + 2)
    return pl.pallas_call(
        functools.partial(kernel, n_blk),
        out_shape=jax.ShapeDtypeStruct((width, half), F32),
        in_specs=[vmem] * 5,
        out_specs=vmem,
        scratch_shapes=[
            pltpu.VMEM((near, width, half), F32),
            pltpu.VMEM((near, 2, tasks, half), F32),
            pltpu.VMEM((near, 2, tasks, half), F32),
            pltpu.VMEM((2, tasks, rows), F32),
            pltpu.VMEM((2, tasks, rows), F32),
            pltpu.VMEM((rows, KDIM), BF16),
            pltpu.VMEM((rows, 12 * tasks), BF16),
            pltpu.VMEM((near + 1, KDIM, half), BF16),
            pltpu.VMEM((near + 1, 12 * tasks, half), BF16),
            pltpu.VMEM((near + 1, 2 * width + 16, half), BF16),
            pltpu.VMEM((rows, 2 * width + 16), F32),
            pltpu.VMEM((width + 8, half), F32),
            pltpu.VMEM((width + 8, half), F32),
            pltpu.SemaphoreType.DMA((near + 1, 5)),
            pltpu.SemaphoreType.DMA((near + 1, 5)),
        ],
        compiler_params=pltpu.CompilerParams(
            collective_id=0, has_side_effects=True, vmem_limit_bytes=48 * 2**20),
        cost_estimate=pl.CostEstimate(flops=pairs * 128, bytes_accessed=2**20, transcendentals=pairs),
        name="window_grad",
    )(inputs, solved, probes, task_factor, inv_len.reshape(1, width))


def solution(mesh):
    placed = (
        P(None, ("groups", "blk")),
        P("inner", ("groups", "blk")),
        P("inner", ("groups", "blk")),
        P("groups", None),
        P("groups"),
    )
    return jax.shard_map(
        functools.partial(local, mesh.shape["blk"]),
        mesh=mesh,
        in_specs=placed,
        out_specs=P(None, ("groups", "blk", "inner")),
        check_vma=False,
    )
```

profile of v0, /device:TPU:0, one launch (start us, length us, event | category | flops | bytes accessed | tf_op | source)
XLA Modules:
  0.0 44.3 jit_solution(1967540104549408397)
XLA Ops:
  0.0 0.0 copy-start.4
  0.0 0.7 %copy-done.4 = f32[32]{0:T(128)S(1)} copy-done((f32[32]{0:T(128)S(1)}, f32[32]{0:T(128)}, u32[]{:S(2)}) %copy-start.4) | copy-done | bytes 152
  0.7 0.0 copy-start
  0.7 0.9 %copy-done = f32[32,2048]{1,0:T(8,128)S(1)} copy-done((f32[32,2048]{1,0:T(8,128)S(1)}, f32[32,2048]{1,0:T(8,128)}, u32[]{:S(2)}) %copy-start) | copy-done | bytes 262168
  1.6 0.0 copy-start.1
  1.6 0.8 %copy-done.1 = f32[8,2048]{1,0:T(8,128)S(1)} copy-done((f32[8,2048]{1,0:T(8,128)S(1)}, f32[8,2048]{1,0:T(8,128)}, u32[]{:S(2)}) %copy-start.1) | copy-done | bytes 65560
  2.4 0.0 copy-start.2
  2.4 0.8 %copy-done.2 = f32[8,2048]{1,0:T(8,128)S(1)} copy-done((f32[8,2048]{1,0:T(8,128)S(1)}, f32[8,2048]{1,0:T(8,128)}, u32[]{:S(2)}) %copy-start.2) | copy-done | bytes 65560
  3.3 0.0 copy-start.3
  3.3 0.7 %copy-done.3 = f32[8,8]{1,0:T(8,128)S(1)} copy-done((f32[8,8]{1,0:T(8,128)S(1)}, f32[8,8]{1,0:T(8,128)}, u32[]{:S(2)}) %copy-start.3) | copy-done | bytes 280
  4.0 39.7 %window_grad.1 = f32[32,1024]{1,0:T(8,128)S(1)} custom-call(f32[32,2048]{1,0:T(8,128)S(1)} %copy-done, f32[8,2048]{1,0:T(8,128)S(1)} %copy-done.1, f32[8,2048]{1,0:T(8,128)S(1)} %copy-done.2, f32[8,8]{1,0:T(8,128)S(1)} %copy-done.3, f32[1,32]{1,0:T(1,128)S(1)} %bitcast.1), custom_call_target="tpu_custom_call" | custom-call | flops 5368709120 | bytes 1048576 | tf_op jit(solution)/shard_map/window_grad/pallas_call | solution.py:202
  43.7 0.7 %copy.7 = f32[32,1024]{1,0:T(8,128)} copy(f32[32,1024]{1,0:T(8,128)S(1)} %window_grad.1) | data formatting | bytes 262144
Async XLA Ops:
  0.0 0.7 %copy-start.4 = (f32[32]{0:T(128)S(1)}, f32[32]{0:T(128)}, u32[]{:S(2)}) copy-start(f32[32]{0:T(128)} %param.9) | copy-start | bytes 388
  0.7 0.9 %copy-start = (f32[32,2048]{1,0:T(8,128)S(1)}, f32[32,2048]{1,0:T(8,128)}, u32[]{:S(2)}) copy-start(f32[32,2048]{1,0:T(8,128)} %x_ref.1) | copy-start | bytes 786436
  1.6 0.8 %copy-start.1 = (f32[8,2048]{1,0:T(8,128)S(1)}, f32[8,2048]{1,0:T(8,128)}, u32[]{:S(2)}) copy-start(f32[8,2048]{1,0:T(8,128)} %u_ref.1) | copy-start | bytes 196612
  2.4 0.8 %copy-start.2 = (f32[8,2048]{1,0:T(8,128)S(1)}, f32[8,2048]{1,0:T(8,128)}, u32[]{:S(2)}) copy-start(f32[8,2048]{1,0:T(8,128)} %v_ref.1) | copy-start | bytes 196612
  3.3 0.7 %copy-start.3 = (f32[8,8]{1,0:T(8,128)S(1)}, f32[8,8]{1,0:T(8,128)}, u32[]{:S(2)}) copy-start(f32[8,8]{1,0:T(8,128)} %f_ref.1) | copy-start | bytes 772
where the time goes:
time: 44.6 us; the launch traced here: 44.3 us
  Pallas kernels  39.7 us (89%)
  local copies, waits for them, and re-layouts  4.63 us (10%)
    pallas_call x1, Pallas kernels, local(): pl.pallas_call(functools.partial(kernel, n_blk), out_shape=jax.ShapeDtype...  39.7 us
    unnamed x11, local copies, waits for them, and re-layouts  4.63 us

commit v1 on v0

--- a/solution.py
+++ b/solution.py
@@ -9,8 +9,8 @@
 from jax.sharding import PartitionSpec as P
 
 PROBES = 2
-OFFSETS = (1, -1, 2, -2)
-TI = 512
+NEAR = 4
+TI = 1024
 JC = 256
 KDIM = 128
 MESH = pl.DeviceIdType.MESH
@@ -32,24 +32,38 @@
     return high, mid, (rest - mid).astype(BF16).astype(F32)
 
 
-def kernel(n_blk, x_ref, u_ref, v_ref, f_ref, len_ref, out_ref,
-           xs, us, vs, own_u, own_v, a_exp, a_pair, b_exp, b_pair, b_y, acc, part, got,
-           send_sem, recv_sem):
+def kernel(n_blk, x_hbm, u_hbm, v_hbm, f_hbm, len_hbm, out_ref,
+           x_ref, f_ref, len_ref, xs, us, vs, own_u, own_v, a_exp, a_pair, b_exp, b_pair, b_y, acc, part, got,
+           send_sem, recv_sem, local_sem):
     grp = lax.axis_index("groups")
     blk = lax.axis_index("blk")
     me = lax.axis_index("inner")
     mate = 1 - me
-    width, rows = x_ref.shape
+    width, rows = x_hbm.shape
     half = rows // 2
-    tasks = u_ref.shape[0]
+    tasks = u_hbm.shape[0]
+
+    loads = [
+        pltpu.make_async_copy(src, dst, local_sem.at[i])
+        for i, (src, dst) in enumerate((
+            (len_hbm, len_ref), (x_hbm, x_ref), (f_hbm, f_ref), (u_hbm, own_u.at[me]), (v_hbm, own_v.at[me])))
+    ]
+    for load in loads:
+        load.start()
+
+    side = 1 - 2 * lax.rem(blk, 2)
+    beside = blk + side
+    after = lax.rem(blk + 2, n_blk)
+    before = lax.rem(blk + n_blk - 2, n_blk)
+    far_up = lax.rem(blk + 2 * side + n_blk, n_blk)
+    far_down = lax.rem(blk - 2 * side + n_blk, n_blk)
 
     barrier = pltpu.get_barrier_semaphore()
     pl.semaphore_signal(barrier, inc=1, device_id=(grp, blk, mate), device_id_type=MESH)
-    for off in OFFSETS:
-        other = lax.rem(blk + off + n_blk, n_blk)
+    for other in (beside, after, before):
         for inner in (me, mate):
             pl.semaphore_signal(barrier, inc=1, device_id=(grp, other, inner), device_id_type=MESH)
-    pl.semaphore_wait(barrier, 1 + 2 * len(OFFSETS))
+    pl.semaphore_wait(barrier, 7)
 
     def remote(src, dst, slot, kind, target):
         return pltpu.make_async_remote_copy(
@@ -60,29 +74,31 @@
     theirs = pl.ds(pl.multiple_of(mate * half, half), half)
 
     def copies(slot):
-        far = len(OFFSETS)
-        if isinstance(slot, int) and slot == far:
-            partner = (grp, blk, mate)
-            return [remote(u_ref, own_u.at[me], far, 0, partner), remote(v_ref, own_v.at[me], far, 1, partner)]
-        target = lax.rem(blk - OFFSETS[slot] + n_blk, n_blk) if isinstance(slot, int) else lax.rem(blk + 1, n_blk)
+        if slot == 3:
+            same = (grp, beside, me)
+            return [remote(xs.at[1], xs.at[3], 3, 0, same),
+                    remote(us.at[1], us.at[3], 3, 1, same),
+                    remote(vs.at[1], vs.at[3], 3, 2, same)]
+        target = (beside, far_down, far_up)[slot]
         same, cross = (grp, target, me), (grp, target, mate)
         return [
-            remote(x_ref.at[:, mine], xs.at[slot], slot, 0, same),
-            remote(u_ref.at[:, mine], us.at[slot, me], slot, 1, same),
-            remote(v_ref.at[:, mine], vs.at[slot, me], slot, 2, same),
-            remote(u_ref.at[:, theirs], us.at[slot, me], slot, 3, cross),
-            remote(v_ref.at[:, theirs], vs.at[slot, me], slot, 4, cross),
+            remote(x_hbm.at[:, mine], xs.at[slot], slot, 0, same),
+            remote(u_hbm.at[:, mine], us.at[slot, me], slot, 1, same),
+            remote(v_hbm.at[:, mine], vs.at[slot, me], slot, 2, same),
+            remote(u_hbm.at[:, theirs], us.at[slot, me], slot, 3, cross),
+            remote(v_hbm.at[:, theirs], vs.at[slot, me], slot, 4, cross),
         ]
 
-    partner_copies = copies(len(OFFSETS))
+    partner = (grp, blk, mate)
+    partner_copies = [remote(u_hbm, own_u.at[me], NEAR, 0, partner), remote(v_hbm, own_v.at[me], NEAR, 1, partner)]
     for copy in partner_copies:
         copy.start()
-    for slot in range(len(OFFSETS)):
+    for slot in (1, 0, 2):
         for copy in copies(slot):
             copy.start()
 
-    own_u[me] = u_ref[...]
-    own_v[me] = v_ref[...]
+    for load in loads:
+        load.wait()
     square = (width, width)
     diag = lax.broadcasted_iota(jnp.int32, square, 0) == lax.broadcasted_iota(jnp.int32, square, 1)
     inv = jnp.sum(jnp.where(diag, jnp.broadcast_to(len_ref[...], square), 0.0), axis=1, keepdims=True)
@@ -130,8 +146,11 @@
         copy.wait()
 
     def fold(ref, at):
-        return jnp.concatenate(
-            [jnp.dot(cov, ref[p, :, at], precision=precise, preferred_element_type=F32) for p in range(2)], axis=0)
+        parts = []
+        for p in range(2):
+            value = ref[p, :, at]
+            parts.append(sum(cov[:, t : t + 1] * value[t : t + 1] for t in range(tasks)))
+        return jnp.concatenate(parts, axis=0)
 
     @pl.loop(0, rows // chunk)
     def _(index):
@@ -169,17 +188,20 @@
         flat = acc[pl.ds(pl.multiple_of(start, half), half), :].T
         return flat[:width] + flat[width : 2 * width], flat[2 * width : 2 * width + 8]
 
-    own = len(OFFSETS)
+    own = NEAR
     prepare(own, x_ref[:, mine], own_u[0, :, mine], own_u[1, :, mine], own_v[0, :, mine], own_v[1, :, mine])
     tiles(own, True, mate * half)
     tiles(own, True, me * half)
     swap = remote(part, got, own, 2, (grp, blk, mate))
-    for slot in range(len(OFFSETS)):
+    for slot in range(NEAR):
         for copy in copies(slot):
             copy.wait()
+        if slot == 1:
+            for copy in copies(3):
+                copy.start()
         prepare(slot, xs[slot], us[slot, 0], us[slot, 1], vs[slot, 0], vs[slot, 1])
         tiles(slot, False, mate * half)
-        if slot == len(OFFSETS) - 1:
+        if slot == NEAR - 1:
             moved, total = gather(mate * half)
             part[:width] = moved
             part[width:] = total
@@ -196,15 +218,18 @@
     width, rows = inputs.shape
     tasks = solved.shape[0]
     half = rows // 2
-    near = len(OFFSETS)
+    near = NEAR
     vmem = pl.BlockSpec(memory_space=pltpu.VMEM)
     pairs = 2 * rows * half * (2 * near + 2)
     return pl.pallas_call(
         functools.partial(kernel, n_blk),
         out_shape=jax.ShapeDtypeStruct((width, half), F32),
-        in_specs=[vmem] * 5,
+        in_specs=[pl.BlockSpec(memory_space=pltpu.HBM)] * 5,
         out_specs=vmem,
         scratch_shapes=[
+            pltpu.VMEM((width, rows), F32),
+            pltpu.VMEM((tasks, tasks), F32),
+            pltpu.VMEM((1, width), F32),
             pltpu.VMEM((near, width, half), F32),
             pltpu.VMEM((near, 2, tasks, half), F32),
             pltpu.VMEM((near, 2, tasks, half), F32),
@@ -220,6 +245,7 @@
             pltpu.VMEM((width + 8, half), F32),
             pltpu.SemaphoreType.DMA((near + 1, 5)),
             pltpu.SemaphoreType.DMA((near + 1, 5)),
+            pltpu.SemaphoreType.DMA((5,)),
         ],
         compiler_params=pltpu.CompilerParams(
             collective_id=0, has_side_effects=True, vmem_limit_bytes=48 * 2**20),

time: 44.6 us -> 37.6 us (0.84)
  Pallas kernels: 39.7 us -> 32.6 us
    pallas_call x1, Pallas kernels: 39.7 us -> 32.6 us  [local(): pl.pallas_call(functools.partial(kernel, n_blk), out_shape=jax.ShapeDtype...]
where the time goes in v1:
time: 37.6 us; the launch traced here: 37.3 us
  Pallas kernels  32.6 us (87%)
  local copies, waits for them, and re-layouts  4.63 us (12%)
    pallas_call x1, Pallas kernels, local(): pl.pallas_call(functools.partial(kernel, n_blk), out_shape=jax.ShapeDtype...  32.6 us
    unnamed x11, local copies, waits for them, and re-layouts  4.63 us

profile of v1, /device:TPU:0, one launch (start us, length us, event | category | flops | bytes accessed | tf_op | source)
XLA Modules:
  0.0 37.3 jit_solution(4043867405202136530)
XLA Ops:
  0.0 0.0 copy-start.4
  0.0 0.7 %copy-done.4 = f32[32]{0:T(128)S(1)} copy-done((f32[32]{0:T(128)S(1)}, f32[32]{0:T(128)}, u32[]{:S(2)}) %copy-start.4) | copy-done | bytes 152
  0.7 0.0 copy-start
  0.7 0.9 %copy-done = f32[32,2048]{1,0:T(8,128)S(1)} copy-done((f32[32,2048]{1,0:T(8,128)S(1)}, f32[32,2048]{1,0:T(8,128)}, u32[]{:S(2)}) %copy-start) | copy-done | bytes 262168
  1.6 0.0 copy-start.1
  1.6 0.8 %copy-done.1 = f32[8,2048]{1,0:T(8,128)S(1)} copy-done((f32[8,2048]{1,0:T(8,128)S(1)}, f32[8,2048]{1,0:T(8,128)}, u32[]{:S(2)}) %copy-start.1) | copy-done | bytes 65560
  2.4 0.0 copy-start.2
  2.4 0.8 %copy-done.2 = f32[8,2048]{1,0:T(8,128)S(1)} copy-done((f32[8,2048]{1,0:T(8,128)S(1)}, f32[8,2048]{1,0:T(8,128)}, u32[]{:S(2)}) %copy-start.2) | copy-done | bytes 65560
  3.3 0.0 copy-start.3
  3.3 0.7 %copy-done.3 = f32[8,8]{1,0:T(8,128)S(1)} copy-done((f32[8,8]{1,0:T(8,128)S(1)}, f32[8,8]{1,0:T(8,128)}, u32[]{:S(2)}) %copy-start.3) | copy-done | bytes 280
  4.0 32.6 %window_grad.1 = f32[32,1024]{1,0:T(8,128)S(1)} custom-call(f32[32,2048]{1,0:T(8,128)S(1)} %copy-done, f32[8,2048]{1,0:T(8,128)S(1)} %copy-done.1, f32[8,2048]{1,0:T(8,128)S(1)} %copy-done.2, f32[8,8]{1,0:T(8,128)S(1)} %copy-done.3, f32[1,32]{1,0:T(1,128)S(1)} %bitcast.1), custom_call_target="tpu_custom_call" | custom-call | flops 5368709120 | bytes 1048576 | tf_op jit(solution)/shard_map/window_grad/pallas_call | solution.py:224
  36.6 0.7 %copy.7 = f32[32,1024]{1,0:T(8,128)} copy(f32[32,1024]{1,0:T(8,128)S(1)} %window_grad.1) | data formatting | bytes 262144
Async XLA Ops:
  0.0 0.7 %copy-start.4 = (f32[32]{0:T(128)S(1)}, f32[32]{0:T(128)}, u32[]{:S(2)}) copy-start(f32[32]{0:T(128)} %param.9) | copy-start | bytes 388
  0.7 0.9 %copy-start = (f32[32,2048]{1,0:T(8,128)S(1)}, f32[32,2048]{1,0:T(8,128)}, u32[]{:S(2)}) copy-start(f32[32,2048]{1,0:T(8,128)} %x_hbm.1) | copy-start | bytes 786436
  1.6 0.8 %copy-start.1 = (f32[8,2048]{1,0:T(8,128)S(1)}, f32[8,2048]{1,0:T(8,128)}, u32[]{:S(2)}) copy-start(f32[8,2048]{1,0:T(8,128)} %u_hbm.1) | copy-start | bytes 196612
  2.4 0.8 %copy-start.2 = (f32[8,2048]{1,0:T(8,128)S(1)}, f32[8,2048]{1,0:T(8,128)}, u32[]{:S(2)}) copy-start(f32[8,2048]{1,0:T(8,128)} %v_hbm.1) | copy-start | bytes 196612
  3.3 0.7 %copy-start.3 = (f32[8,8]{1,0:T(8,128)S(1)}, f32[8,8]{1,0:T(8,128)}, u32[]{:S(2)}) copy-start(f32[8,8]{1,0:T(8,128)} %f_hbm.1) | copy-start | bytes 772

commit v2 on v1

--- a/solution.py
+++ b/solution.py
@@ -11,7 +11,7 @@
 PROBES = 2
 NEAR = 4
 TI = 1024
-JC = 256
+JC = 512
 KDIM = 128
 MESH = pl.DeviceIdType.MESH
 ROOT = math.sqrt(math.log2(math.e))
@@ -119,14 +119,15 @@
         y = x * scale
         yh, yl = split(y)
         tail = jnp.zeros((KDIM - 3 * width - 8, cols), F32)
-        b_exp[slot] = jnp.concatenate([yh, yl, yh, norm_rows(y, True), tail], axis=0).astype(BF16)
+        b_exp[slot] = jnp.concatenate([yh, yl, yh, norm_rows(y, True), tail], axis=0).T.astype(BF16)
         one = jnp.where(lax.broadcasted_iota(jnp.int32, (16, cols), 0) == 0, 1.0, 0.0)
         b_y[slot] = jnp.concatenate([yh, yl, one], axis=0).astype(BF16)
         u = jnp.concatenate([u0, u1], axis=0)
         v = jnp.concatenate([v0, v1], axis=0)
         uh, ul = split(u)
         vh, vl = split(v)
-        b_pair[slot] = jnp.concatenate([vh, vl, vh, uh, ul, uh], axis=0).astype(BF16)
+        pair = jnp.concatenate([vh, vl, vh, uh, ul, uh, jnp.zeros((KDIM - 12 * tasks, cols), F32)], axis=0)
+        b_pair[slot] = pair.T[:, : 12 * tasks].astype(BF16)
 
     chunk = 512
 
@@ -137,7 +138,7 @@
         yh, yl = split(y)
         tail = jnp.zeros((KDIM - 3 * width - 8, chunk), F32)
         full = jnp.concatenate([yh, yh, yl, norm_rows(y, False), tail], axis=0)
-        a_exp[at, :] = full.T.astype(BF16)
+        a_exp[:, at] = full.astype(BF16)
 
     factor = f_ref[...]
     cov = lax.dot_general(factor, factor, (((1,), (1,)), ((), ())), precision=precise, preferred_element_type=F32)
@@ -158,34 +159,28 @@
         gh, gl = split(fold(own_u, at))
         wh, wl = split(fold(own_v, at))
         full = jnp.concatenate([gh, gh, gl, wh, wh, wl, jnp.zeros((KDIM - 12 * tasks, chunk), F32)], axis=0)
-        a_pair[at, :] = full.T[:, : 12 * tasks].astype(BF16)
+        a_pair[:, at] = full[: 12 * tasks].astype(BF16)
 
     def tiles(slot, first, start):
         @pl.loop(0, half // TI)
         def _(index):
-            at = pl.ds(pl.multiple_of(start + index * TI, TI), TI)
-            le = a_exp[at, :]
-            lp = a_pair[at, :]
-            total = None
-            for c in range(half // JC):
-                cols = pl.ds(c * JC, JC)
-                expo = jnp.dot(le, b_exp[slot, :, cols], preferred_element_type=F32)
-                pair = jnp.dot(lp, b_pair[slot, :, cols], preferred_element_type=F32)
+            left = b_y[slot]
+            for c in range(TI // JC):
+                at = pl.ds(pl.multiple_of(start + index * TI + c * JC, JC), JC)
+                expo = jnp.dot(b_exp[slot], a_exp[:, at], preferred_element_type=F32)
+                pair = jnp.dot(b_pair[slot], a_pair[:, at], preferred_element_type=F32)
                 strength = jnp.exp2(expo) * pair
                 high = strength.astype(BF16)
                 low = (strength - high.astype(F32)).astype(BF16)
-                right = b_y[slot, :, cols]
-                dims = (((1,), (1,)), ((), ()))
-                term = lax.dot_general(high, right, dims, preferred_element_type=F32)
-                term = term + lax.dot_general(low, right, dims, preferred_element_type=F32)
-                total = term if total is None else total + term
-            if first:
-                acc[at, :] = total
-            else:
-                acc[at, :] = acc[at, :] + total
+                total = jnp.dot(left, high, preferred_element_type=F32)
+                total = total + jnp.dot(left, low, preferred_element_type=F32)
+                if first:
+                    acc[:, at] = total
+                else:
+                    acc[:, at] = acc[:, at] + total
 
     def gather(start):
-        flat = acc[pl.ds(pl.multiple_of(start, half), half), :].T
+        flat = acc[:, pl.ds(pl.multiple_of(start, half), half)]
         return flat[:width] + flat[width : 2 * width], flat[2 * width : 2 * width + 8]
 
     own = NEAR
@@ -235,12 +230,12 @@
             pltpu.VMEM((near, 2, tasks, half), F32),
             pltpu.VMEM((2, tasks, rows), F32),
             pltpu.VMEM((2, tasks, rows), F32),
-            pltpu.VMEM((rows, KDIM), BF16),
-            pltpu.VMEM((rows, 12 * tasks), BF16),
-            pltpu.VMEM((near + 1, KDIM, half), BF16),
-            pltpu.VMEM((near + 1, 12 * tasks, half), BF16),
+            pltpu.VMEM((KDIM, rows), BF16),
+            pltpu.VMEM((12 * tasks, rows), BF16),
+            pltpu.VMEM((near + 1, half, KDIM), BF16),
+            pltpu.VMEM((near + 1, half, 12 * tasks), BF16),
             pltpu.VMEM((near + 1, 2 * width + 16, half), BF16),
-            pltpu.VMEM((rows, 2 * width + 16), F32),
+            pltpu.VMEM((2 * width + 16, rows), F32),
             pltpu.VMEM((width + 8, half), F32),
             pltpu.VMEM((width + 8, half), F32),
             pltpu.SemaphoreType.DMA((near + 1, 5)),

time: 37.6 us -> 34.7 us (0.923)
  Pallas kernels: 32.6 us -> 29.8 us
    pallas_call x1, Pallas kernels: 32.6 us -> 29.8 us  [local(): pl.pallas_call(functools.partial(kernel, n_blk), out_shape=jax.ShapeDtype...]
where the time goes in v2:
time: 34.7 us; the launch traced here: 34.4 us
  Pallas kernels  29.8 us (86%)
  local copies, waits for them, and re-layouts  4.63 us (13%)
    pallas_call x1, Pallas kernels, local(): pl.pallas_call(functools.partial(kernel, n_blk), out_shape=jax.ShapeDtype...  29.8 us
    unnamed x11, local copies, waits for them, and re-layouts  4.63 us

profile of v2, /device:TPU:0, one launch (start us, length us, event | category | flops | bytes accessed | tf_op | source)
XLA Modules:
  0.0 34.4 jit_solution(12832974543721554571)
XLA Ops:
  0.0 0.0 copy-start.4
  0.0 0.7 %copy-done.4 = f32[32]{0:T(128)S(1)} copy-done((f32[32]{0:T(128)S(1)}, f32[32]{0:T(128)}, u32[]{:S(2)}) %copy-start.4) | copy-done | bytes 152
  0.7 0.0 copy-start
  0.7 0.9 %copy-done = f32[32,2048]{1,0:T(8,128)S(1)} copy-done((f32[32,2048]{1,0:T(8,128)S(1)}, f32[32,2048]{1,0:T(8,128)}, u32[]{:S(2)}) %copy-start) | copy-done | bytes 262168
  1.6 0.0 copy-start.1
  1.6 0.8 %copy-done.1 = f32[8,2048]{1,0:T(8,128)S(1)} copy-done((f32[8,2048]{1,0:T(8,128)S(1)}, f32[8,2048]{1,0:T(8,128)}, u32[]{:S(2)}) %copy-start.1) | copy-done | bytes 65560
  2.4 0.0 copy-start.2
  2.4 0.8 %copy-done.2 = f32[8,2048]{1,0:T(8,128)S(1)} copy-done((f32[8,2048]{1,0:T(8,128)S(1)}, f32[8,2048]{1,0:T(8,128)}, u32[]{:S(2)}) %copy-start.2) | copy-done | bytes 65560
  3.3 0.0 copy-start.3
  3.3 0.7 %copy-done.3 = f32[8,8]{1,0:T(8,128)S(1)} copy-done((f32[8,8]{1,0:T(8,128)S(1)}, f32[8,8]{1,0:T(8,128)}, u32[]{:S(2)}) %copy-start.3) | copy-done | bytes 280
  4.0 29.8 %window_grad.1 = f32[32,1024]{1,0:T(8,128)S(1)} custom-call(f32[32,2048]{1,0:T(8,128)S(1)} %copy-done, f32[8,2048]{1,0:T(8,128)S(1)} %copy-done.1, f32[8,2048]{1,0:T(8,128)S(1)} %copy-done.2, f32[8,8]{1,0:T(8,128)S(1)} %copy-done.3, f32[1,32]{1,0:T(1,128)S(1)} %bitcast.1), custom_call_target="tpu_custom_call" | custom-call | flops 5368709120 | bytes 1048576 | tf_op jit(solution)/shard_map/window_grad/pallas_call | solution.py:219
  33.8 0.7 %copy.7 = f32[32,1024]{1,0:T(8,128)} copy(f32[32,1024]{1,0:T(8,128)S(1)} %window_grad.1) | data formatting | bytes 262144
Async XLA Ops:
  0.0 0.7 %copy-start.4 = (f32[32]{0:T(128)S(1)}, f32[32]{0:T(128)}, u32[]{:S(2)}) copy-start(f32[32]{0:T(128)} %param.9) | copy-start | bytes 388
  0.7 0.9 %copy-start = (f32[32,2048]{1,0:T(8,128)S(1)}, f32[32,2048]{1,0:T(8,128)}, u32[]{:S(2)}) copy-start(f32[32,2048]{1,0:T(8,128)} %x_hbm.1) | copy-start | bytes 786436
  1.6 0.8 %copy-start.1 = (f32[8,2048]{1,0:T(8,128)S(1)}, f32[8,2048]{1,0:T(8,128)}, u32[]{:S(2)}) copy-start(f32[8,2048]{1,0:T(8,128)} %u_hbm.1) | copy-start | bytes 196612
  2.4 0.8 %copy-start.2 = (f32[8,2048]{1,0:T(8,128)S(1)}, f32[8,2048]{1,0:T(8,128)}, u32[]{:S(2)}) copy-start(f32[8,2048]{1,0:T(8,128)} %v_hbm.1) | copy-start | bytes 196612
  3.3 0.7 %copy-start.3 = (f32[8,8]{1,0:T(8,128)S(1)}, f32[8,8]{1,0:T(8,128)}, u32[]{:S(2)}) copy-start(f32[8,8]{1,0:T(8,128)} %f_hbm.1) | copy-start | bytes 772
